TPU v7x, 512 devices: a whole 4x8x8 slice. The times are simulated.
512 devices in a mesh: member: 4 (over x), shard: 128 (over y, z, core).
Axes of the slice: x: 4, y: 8, z: 8, core: 2. Of those that a mesh axis runs over, the one named last changes fastest.
Arguments:
- teacher_hidden: bfloat16 [4, 2048, 4096], P('member', 'shard'), may hold values from -80 to 80
- teacher_gain: float32 [4, 4096], P('member'), may hold values from 0.1 to 1.9
- teacher_head: bfloat16 [4, 4096, 65536], P('member', None, 'shard'), may hold values from -0.5 to 0.5
- student_hidden: bfloat16 [2048, 2048], P('shard', 'member'), may hold values from -8 to 8
- student_head: bfloat16 [2048, 65536], P('member', 'shard'), may hold values from -0.6 to 0.6
- positions: int32 [128, 4], P('shard'), may hold values from 0 to 15, as said below
- counts: int32 [128], replicated, may hold values from 1 to 4, 256 in all
- targets: int32 [512], replicated, may hold values from 0 to 65535
Outputs:
- mean_loss: float32 [], replicated
- hidden_grad: bfloat16 [2048, 2048], P('shard', 'member')
Inputs may be any that keep to these rules, and one draw needn't show every extreme that they name: Each owner's positions are distinct. The counts sum to exactly 256.
All inputs are finite; a program needn't handle non-finite values.
Results may differ from a plain program's by a relative error of at most 0.0039.
Values may be sent and summed in bfloat16 or wider, within the bound.
No kernel may reach another device: no remote copies, remote signals or barrier semaphores. Data moves between devices by JAX's collectives and lax.ppermute only.
A program may use at most 64 MiB of HBM per device.

v0:
```python
import jax
import jax.numpy as jnp
from jax import lax
from jax.sharding import PartitionSpec as P

LOSS_SCALE = 16.0
BLEND = 0.5
EPS = 1e-05


def vocab_stats(logits):
    local_top = jnp.max(logits, axis=1)
    highest = lax.pmax(local_top, "shard")
    totals = lax.psum(jnp.sum(jnp.exp(logits - highest[:, None]), axis=1), "shard")
    return (highest, totals)


def on_device(
    teacher_hidden,
    teacher_gain,
    teacher_head,
    student_hidden,
    student_head,
    positions,
    counts,
    targets,
):
    owners = lax.axis_size("shard")
    members = lax.axis_size("member")
    owner_rank = lax.axis_index("shard")
    slot_ids = positions[0]
    per_owner = slot_ids.shape[0]
    vocab_part = student_head.shape[1]
    window_rows = student_hidden.shape[0]
    widened = jnp.take(teacher_hidden[0], slot_ids, axis=0).astype(jnp.float32)
    inverse_rms = lax.rsqrt(jnp.mean(widened * widened, axis=1, keepdims=True) + EPS)
    normed = (widened * inverse_rms * teacher_gain[0][None, :]).astype(jnp.bfloat16)
    student_picked = jnp.take(student_hidden, slot_ids, axis=0)
    teacher_rows, student_rows = (
        lax.all_gather(normed, "shard", axis=0, tiled=True),
        lax.all_gather(student_picked, "shard", axis=0, tiled=True),
    )
    padded_rows = per_owner * owners
    padded_ids = jnp.arange(padded_rows, dtype=jnp.int32)
    padded_slot = padded_ids % per_owner
    owner_counts = jnp.repeat(counts, per_owner, total_repeat_length=padded_rows)
    padded_weight = (padded_slot < owner_counts).astype(jnp.float32)
    teacher_logits = jnp.dot(teacher_rows, teacher_head[0], preferred_element_type=jnp.float32)
    highest, totals = vocab_stats(teacher_logits)
    teacher_probs = jnp.exp(teacher_logits - highest[:, None]) / totals[:, None]
    partial_logits = jnp.dot(student_rows, student_head, preferred_element_type=jnp.float32)
    student_logits, prob_sums = lax.psum((partial_logits, teacher_probs), "member")
    mean_probs = prob_sums / members
    highest, totals = vocab_stats(student_logits)
    log_total = highest + jnp.log(totals)
    vocab_ids = owner_rank * vocab_part + jnp.arange(vocab_part, dtype=jnp.int32)
    onehot = (vocab_ids[None, :] == targets[:, None]).astype(jnp.float32)
    mixture = BLEND * onehot + (1.0 - BLEND) * mean_probs
    cross_part = jnp.sum(padded_weight * jnp.sum(mixture * student_logits, axis=1))
    lse_part = jnp.where(owner_rank == 0, jnp.sum(padded_weight * log_total), 0.0)
    loss_term = lse_part - cross_part
    slope_rows = (
        LOSS_SCALE
        * padded_weight[:, None]
        * (jnp.exp(student_logits - log_total[:, None]) - mixture)
    ).astype(jnp.bfloat16)
    loss_total = lax.psum(loss_term, "shard")
    mean_loss = loss_total / jnp.sum(counts).astype(jnp.float32)
    chosen = lax.slice_in_dim(slope_rows, 0, per_owner * lax.axis_size("shard"), axis=0)
    slot_grad = lax.psum_scatter(
        lax.dot_general(
            chosen, student_head, (((1,), (1,)), ((), ())), preferred_element_type=jnp.float32
        ),
        "shard",
        scatter_dimension=0,
        tiled=True,
    )
    placed = (jnp.arange(window_rows, dtype=jnp.int32)[:, None] == slot_ids[None, :]).astype(
        jnp.float32
    )
    hidden_grad = jnp.sum(placed[:, :, None] * slot_grad[None, :, :], axis=1).astype(jnp.bfloat16)
    return (mean_loss, hidden_grad)


def solution(mesh):
    placed = (
        P("member", "shard", None),
        P("member", None),
        P("member", None, "shard"),
        P("shard", "member"),
        P("member", "shard"),
        P("shard", None),
        P(),
        P(),
    )
    return jax.shard_map(
        on_device,
        mesh=mesh,
        in_specs=placed,
        out_specs=(P(), P("shard", "member")),
        check_vma=False,
    )
```

profile of v0, /device:TPU:1, one launch (start us, length us, event | category | flops | bytes accessed | tf_op | source)
XLA Modules:
  0.0 1239.3 jit_solution(6478698741609276838)
XLA Ops:
  8.0 0.0 copy-start
  8.0 0.0 copy-start.3
  8.0 0.0 copy-start.4
  8.0 0.0 all-reduce.6.cloned.1.call-start
  8.1 0.7 fusion.23
  8.8 0.7 compare_and_fusion
  9.5 1.3 gather_fusion.1
  10.7 0.1 select_bitcast_fusion
  10.8 58.9 %all-gather = bf16[128,4,512]{2,1,0:T(4,128)(2,1)S(1)} all-gather(bf16[1,4,512]{2,1,0:T(4,128)(2,1)S(1)} %select_bitcast_fusion), channel_id=1, replica_groups=mesh['member'=4,'shard'=128] {'shard'}, dimensions={0}, use_global_device_ids=true | all-gather | bytes 528384 | tf_op jit(solution)/shard_map/all_gather | solution.py:41
  69.8 0.1 reshape.234
  69.9 0.0 copy-done
  69.9 1.4 fusion.29
  71.3 0.0 all-reduce.6.cloned.1.call-update
  71.3 0.0 all-gather.4.cloned.1.call-start
  71.4 0.0 copy-done.3
  71.4 0.6 gather_fusion.2
  72.0 0.2 fusion.12
  72.2 0.0 copy-done.4
  72.2 0.7 fusion.15
  72.9 0.0 all-gather.4.cloned.1.call-update
  72.9 0.0 all-reduce.8.cloned.1.call-start
  73.0 48.6 %all-reduce.6.cloned.1.call-done = f32[512,512]{1,0:T(8,128)} async-done(((f32[512,512]{1,0:T(8,128)}), f32[512,512]{1,0:T(8,128)}) %all-reduce.6.cloned.1.call-update) | async-done | bytes 1048592 | tf_op jit(solution)/shard_map/psum | solution.py:52
  121.6 1.4 reduce_max.18
  123.0 32.7 %all-gather.4.cloned.1.call-done = bf16[128,4,4096]{2,1,0:T(4,128)(2,1)} async-done(((bf16[1,4,4096]{2,1,0:T(4,128)(2,1)}), bf16[128,4,4096]{2,1,0:T(4,128)(2,1)}) %all-gather.4.cloned.1.call-update) | async-done | bytes 4194320 | tf_op jit(solution)/shard_map/all_gather | solution.py:40
  155.6 6.9 reshape.236
  162.6 6.8 fusion.28
  169.4 0.0 copy-start.6
  169.4 0.0 copy-start.1
  169.4 0.0 copy-start.2
  169.4 0.0 copy-start.5
  169.4 1.6 copy.13
  171.1 246.4 %all-reduce.1 = (f32[512]{0:T(512)S(1)}, f32[512]{0:T(512)S(1)}) all-reduce(f32[512]{0:T(512)S(1)} %reduce_max.18, f32[512]{0:T(512)S(1)} %get-tuple-element.25), channel_id=1, replica_groups=mesh['member'=4,'shard'=128] {'shard'}, use_global_device_ids=true, to_apply=%region_2.3 | all-reduce | flops 1024 | bytes 8192 | tf_op jit(solution)/shard_map/pmax | solution.py:13
  417.5 0.3 fusion.3
  417.8 249.4 %psum.37 = f32[512]{0:T(512)S(1)} all-reduce(f32[512]{0:T(512)S(1)} %fusion.3), channel_id=1, replica_groups=mesh['member'=4,'shard'=128] {'shard'}, use_global_device_ids=true, to_apply=%region_10.11 | all-reduce | flops 512 | bytes 4096 | tf_op jit(solution)/shard_map/psum | solution.py:14
  667.2 1.3 fusion.2
  668.4 0.0 all-reduce.8.cloned.1.call-update
  668.5 0.0 all-reduce.10.cloned.1.call-start
  668.5 0.0 copy-done.6
  668.5 0.1 add_add_fusion.1
  668.6 0.0 copy-done.1
  668.6 0.0 copy-start.7
  668.7 3.3 gather_fusion
  672.0 46.3 %all-reduce.8.cloned.1.call-done = f32[512,512]{1,0:T(8,128)} async-done(((f32[512,512]{1,0:T(8,128)}), f32[512,512]{1,0:T(8,128)}) %all-reduce.8.cloned.1.call-update) | async-done | bytes 1048592 | tf_op jit(solution)/shard_map/psum | solution.py:52
  718.4 0.0 copy-done.2
  718.4 0.0 copy-done.5
  718.4 1.8 multiply_reduce_fusion
  720.1 249.5 %psum.36 = f32[512]{0:T(512)S(1)} all-reduce(f32[512]{0:T(512)S(1)} %get-tuple-element.15), channel_id=1, replica_groups=mesh['member'=4,'shard'=128] {'shard'}, use_global_device_ids=true, to_apply=%region_4.5 | all-reduce | flops 512 | bytes 4096 | tf_op jit(solution)/shard_map/psum | solution.py:14
  969.6 0.6 broadcast_select_fusion.1
  970.2 0.6 select_reduce_fusion.1
  970.9 2.8 fusion.4
  973.7 0.0 all-reduce.10.cloned.1.call-update
  973.7 0.6 reduce_sum.78
  975.0 1.3 dynamic-slice.6
  976.3 0.0 copy-done.7
  976.3 0.1 fusion.22
  978.3 250.4 %psum.39 = f32[]{:T(128)} all-reduce(f32[]{:T(128)S(6)} %sub.51), channel_id=1, replica_groups=mesh['member'=4,'shard'=128] {'shard'}, use_global_device_ids=true, to_apply=%region_14.15 | all-reduce | flops 1 | bytes 8 | tf_op jit(solution)/shard_map/psum | solution.py:67
  1229.3 0.0 all-reduce.10.cloned.1.call-done
  1229.4 0.7 constant_dynamic-slice_fusion
  1230.1 0.7 multiply_reduce_fusion.1
  (6 shorter events, 0.0 us)
Async XLA Ops:
  8.0 61.9 %copy-start = (bf16[512,512]{1,0:T(8,128)(2,1)S(1)}, bf16[512,512]{1,0:T(8,128)(2,1)}, u32[]{:S(2)}) copy-start(bf16[512,512]{1,0:T(8,128)(2,1)} %param.14) | copy-start | bytes 1572868
  8.0 63.4 %copy-start.3 = (bf16[1,16,4096]{2,1,0:T(8,128)(2,1)S(1)}, bf16[1,16,4096]{2,1,0:T(8,128)(2,1)}, u32[]{:S(2)}) copy-start(bf16[1,16,4096]{2,1,0:T(8,128)(2,1)} %param.10) | copy-start | bytes 393220
  8.0 64.2 %copy-start.4 = (f32[1,4096]{1,0:T(1,128)S(1)}, f32[1,4096]{1,0:T(1,128)}, u32[]{:S(2)}) copy-start(f32[1,4096]{1,0:T(1,128)} %param.11) | copy-start | bytes 49156
  8.0 113.6 %all-reduce.6.cloned.1.call-start = ((), (), s32[]{:S(2)}) async-start(), calls=%async_computation | async-start | bytes 2097152 | tf_op jit(solution)/shard_map/psum | solution.py:52
  71.3 84.3 %all-gather.4.cloned.1.call-start = ((), (), s32[]{:S(2)}) async-start(), calls=%async_computation.2 | async-start | bytes 4227072 | tf_op jit(solution)/shard_map/all_gather | solution.py:40
  72.9 645.4 %all-reduce.8.cloned.1.call-start = ((), (), s32[]{:S(2)}) async-start(), calls=%async_computation.1 | async-start | bytes 2097152 | tf_op jit(solution)/shard_map/psum | solution.py:52
  169.4 499.2 %copy-start.6 = (s32[4,128]{1,0:T(4,128)S(1)}, s32[4,128]{1,0:T(4,128)}, u32[]{:S(2)}) copy-start(s32[4,128]{1,0:T(4,128)} %constant.159.clone.1) | copy-start | bytes 6148
  169.4 499.3 %copy-start.1 = (s32[128]{0:T(128)S(1)}, s32[128]{0:T(128)}, u32[]{:S(2)}) copy-start(s32[128]{0:T(128)} %param.16) | copy-start | bytes 1540
  169.4 549.0 %copy-start.2 = (f32[512,512]{1,0:T(8,128)S(1)}, f32[512,512]{1,0:T(8,128)}, u32[]{:S(2)}) copy-start(f32[512,512]{1,0:T(8,128)} %all-reduce.6.cloned.1.call-done) | copy-start | bytes 3145732
  169.4 549.0 %copy-start.5 = (s32[512]{0:T(512)S(1)}, s32[512]{0:T(512)}, u32[]{:S(2)}) copy-start(s32[512]{0:T(512)} %param.17) | copy-start | bytes 6148
  668.5 560.9 %all-reduce.10.cloned.1.call-start = ((), (), s32[]{:S(2)}) async-start(), calls=%async_computation.3 | async-start | bytes 2097152
  668.6 307.6 %copy-start.7 = (s32[1,4]{1,0:T(1,128)S(1)}, s32[1,4]{1,0:T(1,128)}, u32[]{:S(2)}) copy-start(s32[1,4]{1,0:T(1,128)} %param.15) | copy-start | bytes 52
Sparse Core Ops, SparseCore 0:
  71.5 50.0 all-reduce.5
  668.6 49.7 all-reduce.7
Sparse Core Ops, SparseCore 1:
  75.4 80.2 all-gather.3
  973.8 190.7 all-reduce.9
where the time goes:
time: 1240 us
  blocking collectives  1050 us (85%)
  waiting for transfers between devices  128 us (10%)
  between operations  20 us (2%)
  local copies, waits for them, and re-layouts  15.9 us (1%)
    psum x2, blocking collectives, vocab_stats(): lax.psum(jnp.sum(jnp.exp(logits - highest[:, None]), axis=1), 'shard')  499 us
    psum x1, blocking collectives, on_device(): loss_total = lax.psum(loss_term, 'shard')  250 us
    pmax x1, blocking collectives, vocab_stats(): highest = lax.pmax(local_top, 'shard')  246 us
    psum x2, waiting for transfers between devices, on_device(): lax.psum((partial_logits, teacher_probs), 'member')  94.9 us
    all_gather x1, blocking collectives, on_device(): lax.all_gather(student_picked, 'shard', axis=0, tiled=True)  58.9 us
    all_gather x1, waiting for transfers between devices, on_device(): lax.all_gather(normed, 'shard', axis=0, tiled=True)  32.7 us
  transfers between devices with their start and end apart: 4, of which 3 were waited for; matrix products, arithmetic and copies ran while one was open for 1% of the time, Pallas kernels for 0%

commit v1 on v0

--- a/solution.py
+++ b/solution.py
@@ -37,7 +37,9 @@
     normed = (widened * inverse_rms * teacher_gain[0][None, :]).astype(jnp.bfloat16)
     student_picked = jnp.take(student_hidden, slot_ids, axis=0)
     teacher_rows, student_rows = (
-        lax.all_gather(normed, "shard", axis=0, tiled=True),
+        jnp.concatenate(
+            lax.all_to_all(jnp.stack([normed] * lax.axis_size("shard")), "shard", 0, 0), axis=0
+        ),
         lax.all_gather(student_picked, "shard", axis=0, tiled=True),
     )
     padded_rows = per_owner * owners

time: 1240 us -> 1320 us (1.065)
  blocking collectives: 1050 us -> 1140 us
  waiting for transfers between devices: 128 us -> 96.6 us
  starting transfers between devices: 0.17 us -> 19.1 us
    all_gather x1, blocking collectives: 58.9 us -> 142 us  [on_device(): lax.all_gather(student_picked, 'shard', axis=0, tiled=True)]
    all_gather x1 -> x0, waiting for transfers between devices: 32.7 us -> none  [on_device(): lax.all_gather(normed, 'shard', axis=0, tiled=True)]
    all_to_all x0 -> x1, starting transfers between devices: none -> 19 us  [on_device(): lax.all_to_all(jnp.stack([normed] * lax.axis_size('shard')), 'shard', 0, 0)]
  transfers between devices with their start and end apart: 4 -> 4, of which waited for: 3 -> 2; matrix products, arithmetic and copies ran while one was open for 1% -> 1% of each run, Pallas kernels for 0% -> 0%
where the time goes in v1:
time: 1320 us
  blocking collectives  1140 us (86%)
  waiting for transfers between devices  96.6 us (7%)
  local copies, waits for them, and re-layouts  20.2 us (2%)
  starting transfers between devices  19.1 us (1%)
  between operations  18.2 us (1%)
    psum x2, blocking collectives, vocab_stats(): lax.psum(jnp.sum(jnp.exp(logits - highest[:, None]), axis=1), 'shard')  499 us
    psum x1, blocking collectives, on_device(): loss_total = lax.psum(loss_term, 'shard')  250 us
    pmax x1, blocking collectives, vocab_stats(): highest = lax.pmax(local_top, 'shard')  249 us
    all_gather x1, blocking collectives, on_device(): lax.all_gather(student_picked, 'shard', axis=0, tiled=True)  142 us
    psum x2, waiting for transfers between devices, on_device(): lax.psum((partial_logits, teacher_probs), 'member')  96.5 us
  transfers between devices with their start and end apart: 4, of which 2 were waited for; matrix products, arithmetic and copies ran while one was open for 1% of the time, Pallas kernels for 0%

profile of v1, /device:TPU:1, one launch (start us, length us, event | category | flops | bytes accessed | tf_op | source)
XLA Modules:
  0.0 1316.1 jit_solution(13777873740725200810)
XLA Ops:
  7.2 0.0 copy-start
  7.2 0.7 fusion.22
  7.9 0.7 compare_and_fusion
  8.6 1.5 gather_fusion.2
  10.1 0.2 fusion.12
  10.3 0.8 fusion.14
  11.1 4.1 stack.2
  15.2 0.0 copy-start.3
  15.2 19.0 %all-to-all-start = ((bf16[128,4,4096]{2,1,0:T(4,128)(2,1)}), bf16[128,4,4096]{2,1,0:T(4,128)(2,1)}, u32[]{:S(2)}, u32[]{:S(2)}) async-start(bf16[128,4,4096]{2,1,0:T(4,128)(2,1)} %stack.2), calls=%async_computation | async-start | bytes 8388608 | tf_op jit(solution)/shard_map/all_to_all | solution.py:41
  34.2 0.0 all-reduce.6.cloned.1.call-start
  34.3 0.0 copy-done.3
  34.3 0.6 gather_fusion.1
  34.9 0.1 select_bitcast_fusion
  34.9 141.7 %all-gather = bf16[128,4,512]{2,1,0:T(4,128)(2,1)S(1)} all-gather(bf16[1,4,512]{2,1,0:T(4,128)(2,1)S(1)} %select_bitcast_fusion), channel_id=1, replica_groups=mesh['member'=4,'shard'=128] {'shard'}, dimensions={0}, use_global_device_ids=true | all-gather | bytes 528384 | tf_op jit(solution)/shard_map/all_gather | solution.py:43
  176.6 0.1 reshape.261
  176.7 0.0 copy-done
  176.7 1.4 fusion.28
  178.2 0.0 all-reduce.6.cloned.1.call-update
  178.2 0.0 all-reduce.8.cloned.1.call-start
  178.2 52.1 %all-reduce.6.cloned.1.call-done = f32[512,512]{1,0:T(8,128)} async-done(((f32[512,512]{1,0:T(8,128)}), f32[512,512]{1,0:T(8,128)}) %all-reduce.6.cloned.1.call-update) | async-done | bytes 1048592 | tf_op jit(solution)/shard_map/psum | solution.py:54
  230.3 1.4 reduce_max.18
  231.7 0.0 all-to-all-done
  231.7 6.9 reshape.235
  238.6 6.8 fusion.27
  245.4 0.0 copy-start.5
  245.4 0.0 copy-start.1
  245.4 0.0 copy-start.2
  245.4 0.0 copy-start.4
  245.5 1.6 copy.13
  247.1 249.5 %all-reduce.1 = (f32[512]{0:T(512)S(1)}, f32[512]{0:T(512)S(1)}) all-reduce(f32[512]{0:T(512)S(1)} %reduce_max.18, f32[512]{0:T(512)S(1)} %get-tuple-element.25), channel_id=1, replica_groups=mesh['member'=4,'shard'=128] {'shard'}, use_global_device_ids=true, to_apply=%region_2.3 | all-reduce | flops 1024 | bytes 8192 | tf_op jit(solution)/shard_map/pmax | solution.py:13
  496.6 0.3 fusion.3
  496.9 249.8 %psum.37 = f32[512]{0:T(512)S(1)} all-reduce(f32[512]{0:T(512)S(1)} %fusion.3), channel_id=1, replica_groups=mesh['member'=4,'shard'=128] {'shard'}, use_global_device_ids=true, to_apply=%region_10.11 | all-reduce | flops 512 | bytes 4096 | tf_op jit(solution)/shard_map/psum | solution.py:14
  746.7 1.3 fusion.2
  748.0 0.0 all-reduce.8.cloned.1.call-update
  748.0 0.0 all-reduce.10.cloned.1.call-start
  748.1 0.0 copy-done.5
  748.1 0.1 add_add_fusion.1
  748.2 0.0 copy-done.1
  748.2 0.0 copy-start.6
  748.2 3.3 gather_fusion
  751.6 44.4 %all-reduce.8.cloned.1.call-done = f32[512,512]{1,0:T(8,128)} async-done(((f32[512,512]{1,0:T(8,128)}), f32[512,512]{1,0:T(8,128)}) %all-reduce.8.cloned.1.call-update) | async-done | bytes 1048592 | tf_op jit(solution)/shard_map/psum | solution.py:54
  796.0 0.0 copy-done.2
  796.0 0.0 copy-done.4
  796.0 1.8 multiply_reduce_fusion
  797.8 249.5 %psum.36 = f32[512]{0:T(512)S(1)} all-reduce(f32[512]{0:T(512)S(1)} %get-tuple-element.15), channel_id=1, replica_groups=mesh['member'=4,'shard'=128] {'shard'}, use_global_device_ids=true, to_apply=%region_4.5 | all-reduce | flops 512 | bytes 4096 | tf_op jit(solution)/shard_map/psum | solution.py:14
  1047.3 0.6 broadcast_select_fusion.1
  1047.9 0.6 select_reduce_fusion.1
  1048.5 2.8 fusion.4
  1051.3 0.0 all-reduce.10.cloned.1.call-update
  1051.4 0.6 reduce_sum.78
  1052.6 1.3 dynamic-slice.6
  1053.9 0.0 copy-done.6
  1053.9 0.1 fusion.21
  1055.9 250.5 %psum.39 = f32[]{:T(128)} all-reduce(f32[]{:T(128)S(6)} %sub.51), channel_id=1, replica_groups=mesh['member'=4,'shard'=128] {'shard'}, use_global_device_ids=true, to_apply=%region_14.15 | all-reduce | flops 1 | bytes 8 | tf_op jit(solution)/shard_map/psum | solution.py:69
  1307.0 0.0 all-reduce.10.cloned.1.call-done
  1307.0 0.7 constant_dynamic-slice_fusion
  1307.8 0.7 multiply_reduce_fusion.1
  (6 shorter events, 0.0 us)
Async XLA Ops:
  7.2 169.6 %copy-start = (bf16[512,512]{1,0:T(8,128)(2,1)S(1)}, bf16[512,512]{1,0:T(8,128)(2,1)}, u32[]{:S(2)}) copy-start(bf16[512,512]{1,0:T(8,128)(2,1)} %param.14) | copy-start | bytes 1572868
  15.2 19.1 %copy-start.3 = (bf16[16,512]{1,0:T(8,128)(2,1)S(1)}, bf16[16,512]{1,0:T(8,128)(2,1)}, u32[]{:S(2)}) copy-start(bf16[16,512]{1,0:T(8,128)(2,1)} %param.13) | copy-start | bytes 49156
  15.2 216.5 %all-to-all-start = ((bf16[128,4,4096]{2,1,0:T(4,128)(2,1)}), bf16[128,4,4096]{2,1,0:T(4,128)(2,1)}, u32[]{:S(2)}, u32[]{:S(2)}) async-start(bf16[128,4,4096]{2,1,0:T(4,128)(2,1)} %stack.2), calls=%async_computation | async-start | bytes 8388608 | tf_op jit(solution)/shard_map/all_to_all | solution.py:41
  34.2 196.1 %all-reduce.6.cloned.1.call-start = ((), (), s32[]{:S(2)}) async-start(), calls=%async_computation.1 | async-start | bytes 2097152 | tf_op jit(solution)/shard_map/psum | solution.py:54
  178.2 617.8 %all-reduce.8.cloned.1.call-start = ((), (), s32[]{:S(2)}) async-start(), calls=%async_computation.2 | async-start | bytes 2097152 | tf_op jit(solution)/shard_map/psum | solution.py:54
  245.4 502.6 %copy-start.5 = (s32[4,128]{1,0:T(4,128)S(1)}, s32[4,128]{1,0:T(4,128)}, u32[]{:S(2)}) copy-start(s32[4,128]{1,0:T(4,128)} %constant.159.clone.1) | copy-start | bytes 6148
  245.4 502.7 %copy-start.1 = (s32[128]{0:T(128)S(1)}, s32[128]{0:T(128)}, u32[]{:S(2)}) copy-start(s32[128]{0:T(128)} %param.16) | copy-start | bytes 1540
  245.4 550.5 %copy-start.2 = (f32[512,512]{1,0:T(8,128)S(1)}, f32[512,512]{1,0:T(8,128)}, u32[]{:S(2)}) copy-start(f32[512,512]{1,0:T(8,128)} %all-reduce.6.cloned.1.call-done) | copy-start | bytes 3145732
  245.4 550.5 %copy-start.4 = (s32[512]{0:T(512)S(1)}, s32[512]{0:T(512)}, u32[]{:S(2)}) copy-start(s32[512]{0:T(512)} %param.17) | copy-start | bytes 6148
  748.0 559.0 %all-reduce.10.cloned.1.call-start = ((), (), s32[]{:S(2)}) async-start(), calls=%async_computation.3 | async-start | bytes 2097152
  748.2 305.7 %copy-start.6 = (s32[1,4]{1,0:T(1,128)S(1)}, s32[1,4]{1,0:T(1,128)}, u32[]{:S(2)}) copy-start(s32[1,4]{1,0:T(1,128)} %param.15) | copy-start | bytes 52
Sparse Core Ops, SparseCore 0:
  178.3 51.9 all-reduce.5
  748.1 47.8 all-reduce.7
  1051.5 191.1 all-reduce.9
